TPU v7x, 32 devices: a whole 2x2x4 slice. The times are simulated.
32 devices in a mesh: dp: 4 (over x, core), tensor: 8 (over z, y).
Axes of the slice: x: 2, y: 2, z: 4, core: 2. Of those that a mesh axis runs over, the one named last changes fastest.
Arguments:
- inputs: bfloat16 [128, 64, 8192], P('dp', None, 'tensor'), may hold values from -6 to 6
- out_grads: bfloat16 [128, 64, 28672], P('dp', None, 'tensor'), may hold values from -6 to 6
- proj_in: bfloat16 [8192, 64], P('tensor'), may hold values from -0.0625 to 0.0625
- proj_out: bfloat16 [28672, 64], P('tensor'), may hold values from -0.03125 to 0.03125
- counts: int32 [128], P(('dp', 'tensor')), may hold values from 1 to 64, as said below
- starts: int32 [128], P(('dp', 'tensor')), may hold values from 0 to 63, as said below
- queries: bfloat16 [1024, 4096], P('dp'), may hold values from -0.01171875 to 0.01171875
Outputs:
- scores: float32 [128, 1024], P(('dp', 'tensor'))
Inputs may be any that keep to these rules, and one draw needn't show every extreme that they name: `counts`: each example holds 1 to 64 tokens; some example holds 64 and some holds 1. starts[e] < counts[e] for every example, so each example has one or more counted positions (weight 1).
All inputs are finite; a program needn't handle non-finite values.
Results may differ from a plain program's by a relative error of at most 0.0029.
Values may be sent and summed in bfloat16 or wider, within the bound.
No kernel may reach another device: no remote copies, remote signals or barrier semaphores. Data moves between devices by JAX's collectives and lax.ppermute only.
A program may use at most 64 MiB of HBM per device.

v0:
```python
import jax
import jax.numpy as jnp
from jax import lax
from jax.sharding import PartitionSpec as P


def body(inputs, out_grads, proj_in, proj_out, counts, starts, queries):
    local_examples = inputs.shape[0]
    length = inputs.shape[1]
    factor_rank = proj_in.shape[1]
    tensor_size = lax.axis_size("tensor")
    owned_count = local_examples // tensor_size
    input_rows = inputs.reshape(local_examples * length, -1)
    grad_rows = out_grads.reshape(local_examples * length, -1)
    in_part = jnp.dot(input_rows, proj_in, preferred_element_type=jnp.float32)
    out_part = jnp.dot(grad_rows, proj_out, preferred_element_type=jnp.float32)
    joined = jnp.concatenate([out_part, in_part], axis=1)
    summed = lax.psum(joined.reshape(local_examples, length, 2 * factor_rank), "tensor")
    owned_rows = lax.dynamic_slice_in_dim(
        summed, lax.axis_index("tensor") * owned_count, owned_count, 0
    )
    position = jnp.arange(length, dtype=jnp.int32)
    weight = (
        (position[None, :] >= starts[:, None]) & (position[None, :] < counts[:, None])
    ).astype(jnp.float32)
    out_proj = owned_rows[:, :, :factor_rank] * weight[:, :, None]
    in_proj = owned_rows[:, :, factor_rank:]
    grads = jnp.einsum("esi,esj->eij", out_proj, in_proj, precision=lax.Precision.HIGHEST)
    grads = grads.reshape(owned_count, factor_rank * factor_rank).astype(jnp.bfloat16)
    return lax.dot_general(
        grads,
        lax.all_gather(queries, "dp", axis=0, tiled=True),
        (((1,), (1,)), ((), ())),
        preferred_element_type=jnp.float32,
    )


def solution(mesh):
    placed = (
        P("dp", None, "tensor"),
        P("dp", None, "tensor"),
        P("tensor", None),
        P("tensor", None),
        P(("dp", "tensor")),
        P(("dp", "tensor")),
        P("dp", None),
    )
    return jax.shard_map(
        body, mesh=mesh, in_specs=placed, out_specs=P(("dp", "tensor"), None), check_vma=False
    )
```

profile of v0, /device:TPU:0, one launch (start us, length us, event | category | flops | bytes accessed | tf_op | source)
XLA Modules:
  0.0 117.3 jit_solution(14592171563289752307)
XLA Ops:
  7.4 0.0 copy-start
  7.4 0.0 all-reduce.2.cloned.1.call-start
  7.4 1.0 copy-done
  8.4 0.0 copy-start.1
  8.4 0.0 copy-start.2
  8.4 9.8 %fusion.5 = f32[2048,64]{0,1:T(8,128)S(1)} fusion(bf16[2048,3584]{1,0:T(8,128)(2,1)} %bitcast.9, bf16[3584,64]{0,1:T(8,128)(2,1)S(1)} %copy-done), kind=kOutput, calls=%fused_computation.10 | convolution fusion | flops 939524096 | bytes 15663104 | tf_op jit(solution)/shard_map/dot_general | solution.py:16
  18.2 0.0 copy-start.3
  18.2 0.0 copy-start.4
  18.2 0.0 copy-done.1
  18.2 0.0 copy-done.2
  18.3 1.4 %fusion.6 = f32[2048,64]{0,1:T(8,128)S(1)} fusion(bf16[2048,1024]{1,0:T(8,128)(2,1)S(1)} %bitcast.10, bf16[1024,64]{0,1:T(8,128)(2,1)S(1)} %copy-done.2), kind=kOutput, calls=%fused_computation.11 | convolution fusion | flops 268435456 | bytes 4849664 | tf_op jit(solution)/shard_map/dot_general | solution.py:15
  19.6 0.1 pad_maximum_fusion
  19.8 1.3 %copy.10 = f32[2048,128]{1,0:T(8,128)} copy(f32[2048,128]{0,1:T(8,128)S(1)} %pad_maximum_fusion) | data formatting | bytes 2097152 | tf_op jit(solution)/shard_map/concatenate | solution.py:17
  21.1 0.0 all-reduce.2.cloned.1.call-update
  21.1 0.0 all-gather.2.cloned.1.call-start
  21.1 0.5 all-gather.2.cloned.1.call-update
  21.7 0.0 copy-done.3
  21.7 0.0 copy-done.4
  21.7 0.1 fusion.3
  21.8 80.2 %all-reduce.2.cloned.1.call-done = f32[32,64,128]{2,1,0:T(8,128)} async-done(((f32[32,64,128]{2,1,0:T(8,128)}), f32[32,64,128]{2,1,0:T(8,128)}) %all-reduce.2.cloned.1.call-update) | async-done | bytes 1048592 | tf_op jit(solution)/shard_map/psum | solution.py:18
  102.0 1.5 %convolution_convert_fusion = bf16[4,64,64]{2,1,0:T(8,128)(2,1)S(1)} fusion(f32[32,64,128]{2,1,0:T(8,128)} %all-reduce.2.cloned.1.call-done, s32[]{:T(128)S(6)} %select_n.3, s32[]{:T(128)S(6)} %add.6, f32[4,64]{1,0:T(4,128)S(1)} %fusion.3), kind=kOutput, calls=%fused_computation | convolution fusion | flops 12615680 | bytes 297472 | tf_op jit(solution)/shard_map/esi,esj->eij/dot_general | solution.py:28
  103.4 0.1 convert_element_type.15
  103.5 0.0 all-gather.2.cloned.1.call-done
  103.6 6.3 %fusion.7 = f32[4,1024]{1,0:T(4,128)} fusion(bf16[4,4096]{1,0:T(4,128)(2,1)S(1)} %convert_element_type.15, bf16[1024,4096]{1,0:T(8,128)(2,1)} %all-gather.2.cloned.1.call-done), kind=kOutput, calls=%fused_computation.12 | convolution fusion | flops 33554432 | bytes 8437760 | tf_op jit(solution)/shard_map/dot_general | solution.py:30
Async XLA Ops:
  7.4 1.0 copy-start
  7.4 94.6 %all-reduce.2.cloned.1.call-start = ((), (), s32[]{:S(2)}) async-start(), calls=%async_computation | async-start | bytes 2097152 | tf_op jit(solution)/shard_map/psum | solution.py:18
  8.4 9.8 %copy-start.1 = (bf16[32,64,1024]{2,1,0:T(8,128)(2,1)S(1)}, bf16[32,64,1024]{2,1,0:T(8,128)(2,1)}, u32[]{:S(2)}) copy-start(bf16[32,64,1024]{2,1,0:T(8,128)(2,1)} %param.7) | copy-start | bytes 12582916
  8.4 9.9 %copy-start.2 = (bf16[1024,64]{0,1:T(8,128)(2,1)S(1)}, bf16[1024,64]{0,1:T(8,128)(2,1)}, u32[]{:S(2)}) copy-start(bf16[1024,64]{0,1:T(8,128)(2,1)} %param.9) | copy-start | bytes 393220
  18.2 3.5 %copy-start.3 = (s32[4]{0:T(128)S(1)}, s32[4]{0:T(128)}, u32[]{:S(2)}) copy-start(s32[4]{0:T(128)} %param.11) | copy-start | bytes 52
  18.2 3.5 %copy-start.4 = (s32[4]{0:T(128)S(1)}, s32[4]{0:T(128)}, u32[]{:S(2)}) copy-start(s32[4]{0:T(128)} %param.12) | copy-start | bytes 52
  21.1 82.5 %all-gather.2.cloned.1.call-start = ((), (), s32[]{:S(2)}) async-start(), calls=%async_computation.1 | async-start | bytes 10485760 | tf_op jit(solution)/shard_map/all_gather | solution.py:32
Sparse Core Ops, SparseCore 0:
  21.2 80.7 all-reduce.1
Sparse Core Ops, SparseCore 1:
  23.2 60.8 all-gather.1
where the time goes:
time: 117 us
  waiting for transfers between devices  80.8 us (69%)
  matrix products  18.9 us (16%)
  between operations  14.9 us (13%)
  local copies, waits for them, and re-layouts  2.44 us (2%)
    psum x1, waiting for transfers between devices, body(): lax.psum(joined.reshape(local_examples, length, 2 * factor_rank), 'tensor')  80.2 us
    dot_general x1, matrix products, body(): out_part = jnp.dot(grad_rows, proj_out, preferred_element_type=jnp.float32)  9.82 us
    dot_general x1, matrix products, body(): lax.dot_general(grads, lax.all_gather(queries, 'dp', axis=0, tiled=True),...  6.26 us
  transfers between devices with their start and end apart: 2, of which 1 were waited for; matrix products, arithmetic and copies ran while one was open for 1% of the time, Pallas kernels for 0%

commit v1 on v0

v1 whole, which is shorter than its diff:
```python
import functools
import math

import jax
import jax.numpy as jnp
from jax import lax
from jax.experimental import pallas as pl
from jax.experimental.pallas import tpu as pltpu
from jax.sharding import PartitionSpec as P

DATA_BOUND = 6.0
IN_BOUND = 0.0625
OUT_BOUND = 0.03125
CONTRACT_LAST = (((1,), (1,)), ((), ()))
VMEM_LIMIT = 20 * 1024 * 1024
BLOCK = 1024
FLIGHT = 5


def code_scale(largest):
    return 2.0 ** math.floor(math.log2(65504.0 / (1.01 * largest**0.25)))


def encode(value, scale):
    root = jnp.sqrt(jnp.sqrt(jnp.abs(value))) * scale
    return jnp.where(value < 0, -root, root)


def decode(code, scale):
    code = code * (1.0 / scale)
    square = code * code
    return jnp.where(code < 0, -square * square, square * square)


def project_kernel(offsets, away, first, scale, grads_hbm, inputs_hbm, out_factor, in_factor, *refs):
    refs = list(refs)
    queries_hbm = refs.pop(0) if first else None
    home = len(offsets) - away
    results = [refs.pop(0) for n in (home, away) if n > 0]
    out_held, in_held, queries = (refs.pop(0), refs.pop(0), refs.pop(0)) if first else (out_factor, in_factor, None)
    grads, inputs, sems, extra_sems = refs
    count, chunk, wide = grads.shape
    narrow = inputs.shape[2]
    rank = out_held.shape[0]
    me = lax.axis_index("tensor")
    blocks = [(start, min(BLOCK, wide - start)) for start in range(0, wide, BLOCK)]
    teams = [range(g, min(g + 2, count)) for g in range(0, count, 2)]

    queue = []
    for team in teams:
        for n, (start, width) in enumerate([(0, narrow)] + blocks):
            source, target = (inputs_hbm, inputs) if n == 0 else (grads_hbm, grads)
            queue.append(
                [
                    pltpu.make_async_copy(
                        source.at[pl.ds(pl.multiple_of((me ^ offsets[g]) * chunk, chunk), chunk), pl.ds(start, width)],
                        target.at[g, :, pl.ds(start, width)],
                        sems.at[g, n],
                    )
                    for g in team
                ]
            )
    loads = []
    if first:
        queue.append([pltpu.make_async_copy(queries_hbm, queries, extra_sems.at[2])])
        loads = [
            pltpu.make_async_copy(in_factor, in_held, extra_sems.at[0]),
            pltpu.make_async_copy(out_factor, out_held, extra_sems.at[1]),
        ]
    begun = done = 0

    def begin(upto):
        nonlocal begun
        while begun < min(upto, len(queue)):
            for copy in queue[begun]:
                copy.start()
            begun += 1

    def finish():
        nonlocal done
        for copy in queue[done]:
            copy.wait()
        done += 1
        begin(done + FLIGHT)

    if first:
        loads[0].start()
        begin(1)
        loads[1].start()
    begin(FLIGHT - 1)
    for team in teams:
        span = slice(team[0], team[-1] + 1)
        tokens = len(team) * chunk
        finish()
        if first and team[0] == 0:
            loads[0].wait()
        in_part = lax.dot_general(
            in_held[...], inputs[span].reshape(tokens, narrow), CONTRACT_LAST, preferred_element_type=jnp.float32
        )
        out_part = None
        for n, (start, width) in enumerate(blocks):
            finish()
            if first and team[0] == 0 and n == 0:
                loads[1].wait()
            columns = slice(start, start + width)
            part = lax.dot_general(
                out_held[:, columns],
                grads[span, :, columns].reshape(tokens, width),
                CONTRACT_LAST,
                preferred_element_type=jnp.float32,
            )
            out_part = part if n == 0 else out_part + part
        for n, g in enumerate(team):
            lanes = slice(n * chunk, (n + 1) * chunk)
            for rows, half in ((slice(0, rank), out_part[:, lanes]), (slice(rank, 2 * rank), in_part[:, lanes])):
                if g < home:
                    results[0][g, rows, :] = half
                else:
                    results[-1][g - home, rows, :] = encode(half, scale)
    while done < len(queue):
        finish()


def project(grad_rows, input_rows, factors, offsets, away, queries, chunk, scale):
    first = queries is not None
    wide, narrow = grad_rows.shape[1], input_rows.shape[1]
    rank = factors[0].shape[0]
    count = len(offsets)
    data = grad_rows.dtype
    hbm = pl.BlockSpec(memory_space=pltpu.HBM)
    vmem = pl.BlockSpec(memory_space=pltpu.VMEM)

    def pinned(array):
        return pltpu.with_memory_space_constraint(array, pltpu.HBM)

    operands = [pinned(grad_rows), pinned(input_rows)] + [pinned(f) if first else f for f in factors]
    in_specs = [hbm, hbm] + [hbm if first else vmem] * 2
    shapes = [((n, 2 * rank, chunk), jnp.float32) for n in (count - away, away) if n > 0]
    if first:
        operands.append(pinned(queries))
        in_specs.append(hbm)
        shapes += [((rank, wide), data), ((rank, narrow), data), (queries.shape, data)]
    return pl.pallas_call(
        functools.partial(project_kernel, tuple(offsets), away, first, scale),
        in_specs=in_specs,
        out_specs=[vmem] * len(shapes),
        out_shape=[jax.ShapeDtypeStruct(*shape) for shape in shapes],
        scratch_shapes=[
            pltpu.VMEM((count, chunk, wide), data),
            pltpu.VMEM((count, chunk, narrow), data),
            pltpu.SemaphoreType.DMA((count, -(-wide // BLOCK) + 1)),
            pltpu.SemaphoreType.DMA((3,)),
        ],
        compiler_params=pltpu.CompilerParams(vmem_limit_bytes=VMEM_LIMIT),
        cost_estimate=pl.CostEstimate(
            flops=4 * count * chunk * rank * (wide + narrow),
            bytes_accessed=2 * count * chunk * (wide + narrow),
            transcendentals=0,
        ),
        name="project",
    )(*operands)


def hold_kernel(ours, theirs, held, sems):
    pieces = sems.shape[1]
    size = ours.shape[0]
    rows = size // pieces
    core = lax.axis_index("dp") & 1
    copies = []
    for m, source in enumerate((theirs, ours)):
        start = pl.multiple_of((core ^ (1 - m)) * size, size)
        for n in range(pieces):
            copies.append(
                pltpu.make_async_copy(
                    source.at[pl.ds(n * rows, rows)], held.at[pl.ds(start + n * rows, rows)], sems.at[m, n]
                )
            )
    for copy in copies:
        copy.start()
    for copy in copies:
        copy.wait()


def hold(ours, theirs):
    return pl.pallas_call(
        hold_kernel,
        in_specs=[pl.BlockSpec(memory_space=pl.ANY)] * 2,
        out_specs=pl.BlockSpec(memory_space=pltpu.VMEM),
        out_shape=pltpu.VMEM((2 * ours.shape[0], ours.shape[1]), ours.dtype),
        scratch_shapes=[pltpu.SemaphoreType.DMA((2, 4))],
        compiler_params=pltpu.CompilerParams(vmem_limit_bytes=8 * 1024 * 1024),
        cost_estimate=pl.CostEstimate(flops=0, bytes_accessed=4 * ours.size, transcendentals=0),
        name="hold",
    )(ours, theirs)


def body(inputs, out_grads, proj_in, proj_out, counts, starts, queries):
    local_examples = inputs.shape[0]
    length = inputs.shape[1]
    rank = proj_in.shape[1]
    tensor_size = lax.axis_size("tensor")
    dp_size = lax.axis_size("dp")
    owned = local_examples // tensor_size
    chunk = owned * length
    input_rows = inputs.reshape(local_examples * length, -1)
    grad_rows = out_grads.reshape(local_examples * length, -1)
    largest = DATA_BOUND * max(grad_rows.shape[1] * OUT_BOUND, input_rows.shape[1] * IN_BOUND)
    scale, pair_scale = code_scale(largest), code_scale(2 * largest)

    pairs = tensor_size // 2
    far = list(range(pairs - 1, 0, -1))
    partner = [(i, i ^ 1) for i in range(tensor_size)]

    def received(part, coding):
        return decode(part.astype(jnp.float32), coding)

    coded, out_factor, in_factor, queries = project(
        grad_rows, input_rows, (proj_out.T, proj_in.T), [2 * m + 1 for m in far + [0]], pairs, queries, chunk, scale
    )
    got_far = lax.ppermute(coded[:-1].astype(jnp.float16), "tensor", partner)
    (home,) = project(
        grad_rows, input_rows, (out_factor, in_factor), [2 * m for m in far + [0]], 0, None, chunk, scale
    )
    coded_near = coded[-1] + 0.0 * got_far[0].astype(jnp.float32)
    got_near = lax.ppermute(coded_near.astype(jnp.float16), "tensor", partner)
    leaving = encode(home[:-1] + received(got_far, scale), pair_scale).astype(jnp.float16)
    sent = [
        lax.ppermute(leaving[n], "tensor", [(i, i ^ (2 * m)) for i in range(tensor_size)]) for n, m in enumerate(far)
    ]
    total = home[-1] + received(got_near, scale)
    for part in sent:
        total = total + received(part, pair_scale)

    summed = total.T.reshape(owned, length, 2 * rank)
    position = jnp.arange(length, dtype=jnp.int32)
    weight = (
        (position[None, :] >= starts[:, None]) & (position[None, :] < counts[:, None])
    ).astype(jnp.float32)
    out_proj = summed[:, :, :rank] * weight[:, :, None]
    in_proj = summed[:, :, rank:]
    grads = jnp.einsum("esi,esj->eij", out_proj, in_proj, precision=lax.Precision.HIGH)
    grads = grads.reshape(owned, rank * rank).astype(jnp.bfloat16)

    twin = lax.ppermute(queries, "dp", [(i, i ^ 1) for i in range(dp_size)])
    me = lax.axis_index("dp")
    chips = dp_size // 2
    across = [[(i, i ^ (2 * k + 1)) for i in range(dp_size)] for k in range(chips)]
    rows = jnp.concatenate([grads] + [lax.ppermute(grads, "dp", across[k]) for k in range(1, chips)], axis=0)
    scores = lax.dot_general(rows, hold(queries, twin), CONTRACT_LAST, preferred_element_type=jnp.float32)
    scores = scores.reshape(chips, owned, -1)
    blocks = [scores[0]] + [lax.ppermute(scores[k], "dp", across[k]) for k in range(1, chips)]
    chip = me >> 1
    columns = []
    for c in range(chips):
        column = blocks[0]
        for k in range(1, chips):
            column = jnp.where((chip ^ k) == c, blocks[k], column)
        columns.append(column)
    return jnp.concatenate(columns, axis=1)


def solution(mesh):
    placed = (
        P("dp", None, "tensor"),
        P("dp", None, "tensor"),
        P("tensor", None),
        P("tensor", None),
        P(("dp", "tensor")),
        P(("dp", "tensor")),
        P("dp", None),
    )
    return jax.shard_map(
        body, mesh=mesh, in_specs=placed, out_specs=P(("dp", "tensor"), None), check_vma=False
    )
```

time: 117 us -> 33.7 us (0.29)
  waiting for transfers between devices: 80.8 us -> 6.76 us
  matrix products: 18.9 us -> 1.57 us
  between operations: 14.9 us -> 0.07 us
  Pallas kernels: 0 us -> 12.5 us
  starting transfers between devices: 0.05 us -> 11.1 us
  local copies, waits for them, and re-layouts: 2.44 us -> 0.25 us
    psum x1 -> x0, waiting for transfers between devices: 80.2 us -> none  [body(): lax.psum(joined.reshape(local_examples, length, 2 * factor_rank), 'tensor')]
    dot_general x4 -> x2, matrix products: 18.9 us -> 1.57 us  [the longest x1 1.18 us: body(): lax.dot_general(rows, hold(queries, twin), CONTRACT_LAST, preferred_eleme...]
    pallas_call x0 -> x3, Pallas kernels: none -> 12.5 us  [the longest x2 10.9 us: project(): pl.pallas_call(functools.partial(project_kernel, tuple(offsets), away, fi...]
    ppermute x0 -> x8, starting transfers between devices: none -> 11.1 us  [the longest x3 4.53 us: body(): lax.ppermute(leaving[n], 'tensor', [(i, i ^ 2 * m) for i in range(tensor_...]
    ppermute x0 -> x8, waiting for transfers between devices: none -> 6.76 us  [the longest x3 3.01 us: body(): lax.ppermute(leaving[n], 'tensor', [(i, i ^ 2 * m) for i in range(tensor_...]
    concatenate x1 -> x0, local copies, waits for them, and re-layouts: 1.29 us -> none  [body(): joined = jnp.concatenate([out_part, in_part], axis=1)]
  transfers between devices with their start and end apart: 2 -> 8, of which waited for: 1 -> 5; matrix products, arithmetic and copies ran while one was open for 1% -> 4% of each run, Pallas kernels for 0% -> 20%
where the time goes in v1:
time: 33.7 us; the launch traced here: 33.6 us
  Pallas kernels  12.5 us (37%)
  starting transfers between devices  11.1 us (33%)
  waiting for transfers between devices  6.76 us (20%)
  matrix products  1.57 us (5%)
  other arithmetic  1.28 us (4%)
    pallas_call x2, Pallas kernels, project(): pl.pallas_call(functools.partial(project_kernel, tuple(offsets), away, fi...  10.9 us
    ppermute x3, starting transfers between devices, body(): lax.ppermute(leaving[n], 'tensor', [(i, i ^ 2 * m) for i in range(tensor_...  4.53 us
    ppermute x3, waiting for transfers between devices, body(): lax.ppermute(leaving[n], 'tensor', [(i, i ^ 2 * m) for i in range(tensor_...  3.01 us
    ppermute x1, starting transfers between devices, body(): got_far = lax.ppermute(coded[:-1].astype(jnp.float16), 'tensor', partner)  2.6 us
    ppermute x1, waiting for transfers between devices, body(): lax.ppermute(scores[k], 'dp', across[k])  2.15 us
    ppermute x1, starting transfers between devices, body(): got_near = lax.ppermute(coded_near.astype(jnp.float16), 'tensor', partner)  1.72 us
    pallas_call x1, Pallas kernels, hold(): pl.pallas_call(hold_kernel, in_specs=[pl.BlockSpec(memory_space=pl.ANY)]...  1.59 us
    ppermute x1, waiting for transfers between devices, body(): lax.ppermute(grads, 'dp', across[k])  1.19 us
  transfers between devices with their start and end apart: 8, of which 5 were waited for; matrix products, arithmetic and copies ran while one was open for 4% of the time, Pallas kernels for 20%

profile of v1, /device:TPU:0, one launch (start us, length us, event | category | flops | bytes accessed | tf_op | source)
XLA Modules:
  0.0 33.6 jit_solution(13945719424625610674)
XLA Ops:
  0.0 5.8 %project.2 = (f32[4,128,256]{2,1,0:T(8,128)S(1)}, bf16[64,3584]{1,0:T(8,128)(2,1)S(1)}, bf16[64,1024]{1,0:T(8,128)(2,1)S(1)}, bf16[256,4096]{1,0:T(8,128)(2,1)S(1)}) custom-call(bf16[2048,3584]{1,0:T(8,128)(2,1)} %bitcast.20, bf16[2048,1024]{1,0:T(8,128)(2,1)} %bitcast.22, bf16[64,3584]{1,0:T(8,128)(2,1)} %bitcast.25, bf16[64,1024]{1,0:T(8,128)(2,1)} %bitcast.26, ...), custom_call_target="tpu_custom_call" | custom-call | flops 1207959552 | bytes 9437184 | tf_op jit(solution)/shard_map/project/pallas_call | solution.py:143
  5.8 0.5 %collective-permute-start.6 = (bf16[256,4096]{1,0:T(8,128)(2,1)S(1)}, bf16[256,4096]{1,0:T(8,128)(2,1)}, u32[]{:S(2)}, u32[]{:S(2)}) collective-permute-start(bf16[256,4096]{1,0:T(8,128)(2,1)S(1)} %get-tuple-element.12.ours), channel_id=1, source_target_pairs={{0,8},{8,0},{16,24},{24,16},{1,9},{9,1},{17,25},{25,17},{2,10},{10... | collective-permute-start | bytes 6291464 | tf_op jit(solution)/shard_map/ppermute | solution.py:244
  6.3 2.6 %collective-permute-start = (f16[3,128,256]{2,1,0:T(8,128)(2,1)S(1)}, f16[3,128,256]{2,1,0:T(8,128)(2,1)S(1)}, u32[]{:S(2)}, u32[]{:S(2)}) collective-permute-start(f16[3,128,256]{2,1,0:T(8,128)(2,1)S(1)} %slice_convert_fusion), channel_id=1, source_target_pairs={{0,1},{1,0},{2,3},{3,2},{4,5},{5,4},{6,7},{7,6},{8,9},{9,8},{10,11... | collective-permute-start | bytes 589832 | tf_op jit(solution)/shard_map/ppermute | solution.py:220
  8.9 0.0 copy-start
  8.9 0.0 copy-start.1
  8.9 5.1 %project.3 = f32[4,128,256]{2,1,0:T(8,128)S(1)} custom-call(bf16[2048,3584]{1,0:T(8,128)(2,1)} %bitcast.21, bf16[2048,1024]{1,0:T(8,128)(2,1)} %bitcast.23, bf16[64,3584]{1,0:T(8,128)(2,1)S(1)} %get-tuple-element.9.out_factor, bf16[64,1024]{1,0:T(8,128)(2,1)S(1)} %get-tuple-element.10.in_factor), custom_call_target="tpu_custom_call" | custom-call | flops 1207959552 | bytes 9437184 | tf_op jit(solution)/shard_map/project/pallas_call | solution.py:143
  14.1 0.4 %collective-permute-done = f16[3,128,256]{2,1,0:T(8,128)(2,1)S(1)} collective-permute-done((f16[3,128,256]{2,1,0:T(8,128)(2,1)S(1)}, f16[3,128,256]{2,1,0:T(8,128)(2,1)S(1)}, u32[]{:S(2)}, u32[]{:S(2)}) %collective-permute-start) | collective-permute-done | bytes 196640 | tf_op jit(solution)/shard_map/ppermute | solution.py:220
  14.5 0.4 %fusion.2 = f16[3,128,256]{2,1,0:T(8,128)(2,1)S(1)} fusion(f16[3,128,256]{2,1,0:T(8,128)(2,1)S(1)} %collective-permute-done, f32[4,128,256]{2,1,0:T(8,128)S(1)} %project.3), kind=kLoop, calls=%fused_computation.5 | loop fusion | flops 1474560 | bytes 786432 | tf_op jit(solution)/shard_map/convert_element_type | solution.py:226
  14.9 3.9 %collective-permute-start.2 = (f16[128,256]{1,0:T(8,128)(2,1)S(1)}, f16[128,256]{1,0:T(8,128)(2,1)S(1)}, u32[]{:S(2)}, u32[]{:S(2)}) collective-permute-start(f16[128,256]{1,0:T(8,128)(2,1)S(1)} %get-tuple-element.13), channel_id=1, source_target_pairs={{0,6},{1,7},{2,4},{3,5},{4,2},{5,3},{6,0},{7,1},{8,14},{9,15},{10,... | collective-permute-start | bytes 196616 | tf_op jit(solution)/shard_map/ppermute | solution.py:228
  18.8 0.0 collective-permute-start.3
  18.8 0.6 %collective-permute-start.4 = (f16[128,256]{1,0:T(8,128)(2,1)S(1)}, f16[128,256]{1,0:T(8,128)(2,1)S(1)}, u32[]{:S(2)}, u32[]{:S(2)}) collective-permute-start(f16[128,256]{1,0:T(8,128)(2,1)S(1)} %get-tuple-element.14), channel_id=1, source_target_pairs={{0,2},{1,3},{2,0},{3,1},{4,6},{5,7},{6,4},{7,5},{8,10},{9,11},{10,... | collective-permute-start | bytes 196616 | tf_op jit(solution)/shard_map/ppermute | solution.py:228
  19.5 1.7 %collective-permute-start.1 = (f16[128,256]{1,0:T(8,128)(2,1)S(1)}, f16[128,256]{1,0:T(8,128)(2,1)S(1)}, u32[]{:S(2)}, u32[]{:S(2)}) collective-permute-start(f16[128,256]{1,0:T(8,128)(2,1)S(1)} %fusion.18), channel_id=1, source_target_pairs={{0,1},{1,0},{2,3},{3,2},{4,5},{5,4},{6,7},{7,6},{8,9},{9,8},{10,11... | collective-permute-start | bytes 196616 | tf_op jit(solution)/shard_map/ppermute | solution.py:225
  21.2 0.0 copy-done
  21.2 0.0 copy-done.1
  21.2 0.1 fusion.25
  21.3 0.3 collective-permute-done.2
  21.5 2.7 %collective-permute-done.3 = f16[128,256]{1,0:T(8,128)(2,1)S(1)} collective-permute-done((f16[128,256]{1,0:T(8,128)(2,1)S(1)}, f16[128,256]{1,0:T(8,128)(2,1)S(1)}, u32[]{:S(2)}, u32[]{:S(2)}) %collective-permute-start.3) | collective-permute-done | bytes 65568 | tf_op jit(solution)/shard_map/ppermute | solution.py:228
  24.3 0.0 collective-permute-done.4
  24.3 0.0 collective-permute-done.1
  24.3 0.2 fusion.9
  24.5 0.1 copy.10
  24.6 0.4 %convolution_convert_fusion = bf16[4,64,64]{2,1,0:T(8,128)(2,1)S(1)} fusion(f32[4,64,128]{2,1,0:T(8,128)S(1)} %bitcast.24, f32[4,64]{1,0:T(4,128)S(1)} %fusion.25), kind=kOutput, calls=%fused_computation | convolution fusion | flops 6324224 | bytes 296960 | tf_op jit(solution)/shard_map/esi,esj->eij/dot_general | solution.py:241
  25.0 0.1 convert_element_type.53
  25.1 0.8 %collective-permute-start.5 = (bf16[4,4096]{1,0:T(4,128)(2,1)S(1)}, bf16[4,4096]{1,0:T(4,128)(2,1)S(1)}, u32[]{:S(2)}, u32[]{:S(2)}) collective-permute-start(bf16[4,4096]{1,0:T(4,128)(2,1)S(1)} %convert_element_type.53), channel_id=1, source_target_pairs={{0,24},{8,16},{16,8},{24,0},{1,25},{9,17},{17,9},{25,1},{2,26},{10... | collective-permute-start | bytes 98312 | tf_op jit(solution)/shard_map/ppermute | solution.py:248
  25.9 0.0 collective-permute-done.6.theirs
  25.9 1.6 %hold.1 = bf16[512,4096]{1,0:T(8,128)(2,1)S(1)} custom-call(bf16[256,4096]{1,0:T(8,128)(2,1)S(1)} %get-tuple-element.12.ours, bf16[256,4096]{1,0:T(8,128)(2,1)} %collective-permute-done.6.theirs), custom_call_target="tpu_custom_call" | custom-call | bytes 4194304 | tf_op jit(solution)/shard_map/hold/pallas_call | solution.py:185
  27.5 1.2 %collective-permute-done.5 = bf16[4,4096]{1,0:T(4,128)(2,1)S(1)} collective-permute-done((bf16[4,4096]{1,0:T(4,128)(2,1)S(1)}, bf16[4,4096]{1,0:T(4,128)(2,1)S(1)}, u32[]{:S(2)}, u32[]{:S(2)}) %collective-permute-start.5) | collective-permute-done | bytes 32800 | tf_op jit(solution)/shard_map/ppermute | solution.py:248
  28.7 1.2 %fusion.19 = f32[8,512]{1,0:T(8,128)S(1)} fusion(bf16[512,4096]{1,0:T(8,128)(2,1)S(1)} %hold.1, bf16[4,4096]{1,0:T(4,128)(2,1)S(1)} %collective-permute-done.5, bf16[4,4096]{1,0:T(4,128)(2,1)S(1)} %convert_element_type.53), kind=kOutput, calls=%fused_computation.38 | convolution fusion | flops 33685504 | bytes 4276224 | tf_op jit(solution)/shard_map/dot_general | solution.py:249
  29.9 0.9 %collective-permute-start.7 = (f32[4,512]{1,0:T(4,128)S(1)}, f32[4,512]{1,0:T(4,128)S(1)}, u32[]{:S(2)}, u32[]{:S(2)}) collective-permute-start(f32[4,512]{1,0:T(4,128)S(1)} %slice.60), channel_id=1, source_target_pairs={{0,24},{8,16},{16,8},{24,0},{1,25},{9,17},{17,9},{25,1},{2,26},{10... | collective-permute-start | bytes 24584 | tf_op jit(solution)/shard_map/ppermute | solution.py:251
  30.8 2.1 %collective-permute-done.7 = f32[4,512]{1,0:T(4,128)S(1)} collective-permute-done((f32[4,512]{1,0:T(4,128)S(1)}, f32[4,512]{1,0:T(4,128)S(1)}, u32[]{:S(2)}, u32[]{:S(2)}) %collective-permute-start.7) | collective-permute-done | bytes 8224 | tf_op jit(solution)/shard_map/ppermute | solution.py:251
  33.0 0.6 %pad_maximum_fusion = f32[4,1024]{1,0:T(4,128)} fusion(f32[4,512]{1,0:T(4,128)S(1)} %get-tuple-element.17, f32[4,512]{1,0:T(4,128)S(1)} %get-tuple-element.16), kind=kLoop, calls=%fused_computation.43 | loop fusion | flops 4096 | bytes 32768 | tf_op jit(solution)/shard_map/concatenate | solution.py:259
  (5 shorter events, 0.1 us)
Async XLA Ops:
  5.8 20.1 %collective-permute-start.6 = (bf16[256,4096]{1,0:T(8,128)(2,1)S(1)}, bf16[256,4096]{1,0:T(8,128)(2,1)}, u32[]{:S(2)}, u32[]{:S(2)}) collective-permute-start(bf16[256,4096]{1,0:T(8,128)(2,1)S(1)} %get-tuple-element.12.ours), channel_id=1, source_target_pairs={{0,8},{8,0},{16,24},{24,16},{1,9},{9,1},{17,25},{25,17},{2,10},{10... | collective-permute-start | bytes 6291464 | tf_op jit(solution)/shard_map/ppermute | solution.py:244
  6.3 8.2 %collective-permute-start = (f16[3,128,256]{2,1,0:T(8,128)(2,1)S(1)}, f16[3,128,256]{2,1,0:T(8,128)(2,1)S(1)}, u32[]{:S(2)}, u32[]{:S(2)}) collective-permute-start(f16[3,128,256]{2,1,0:T(8,128)(2,1)S(1)} %slice_convert_fusion), channel_id=1, source_target_pairs={{0,1},{1,0},{2,3},{3,2},{4,5},{5,4},{6,7},{7,6},{8,9},{9,8},{10,11... | collective-permute-start | bytes 589832 | tf_op jit(solution)/shard_map/ppermute | solution.py:220
  8.9 12.3 %copy-start = (s32[4]{0:T(128)S(1)}, s32[4]{0:T(128)}, u32[]{:S(2)}) copy-start(s32[4]{0:T(128)} %param.11) | copy-start | bytes 52
  8.9 12.3 %copy-start.1 = (s32[4]{0:T(128)S(1)}, s32[4]{0:T(128)}, u32[]{:S(2)}) copy-start(s32[4]{0:T(128)} %param.12) | copy-start | bytes 52
  14.9 6.6 %collective-permute-start.2 = (f16[128,256]{1,0:T(8,128)(2,1)S(1)}, f16[128,256]{1,0:T(8,128)(2,1)S(1)}, u32[]{:S(2)}, u32[]{:S(2)}) collective-permute-start(f16[128,256]{1,0:T(8,128)(2,1)S(1)} %get-tuple-element.13), channel_id=1, source_target_pairs={{0,6},{1,7},{2,4},{3,5},{4,2},{5,3},{6,0},{7,1},{8,14},{9,15},{10,... | collective-permute-start | bytes 196616 | tf_op jit(solution)/shard_map/ppermute | solution.py:228
  18.8 5.5 %collective-permute-start.3 = (f16[128,256]{1,0:T(8,128)(2,1)S(1)}, f16[128,256]{1,0:T(8,128)(2,1)S(1)}, u32[]{:S(2)}, u32[]{:S(2)}) collective-permute-start(f16[128,256]{1,0:T(8,128)(2,1)S(1)} %get-tuple-element.15), channel_id=1, source_target_pairs={{0,4},{1,5},{2,6},{3,7},{4,0},{5,1},{6,2},{7,3},{8,12},{9,13},{10,... | collective-permute-start | bytes 196616 | tf_op jit(solution)/shard_map/ppermute | solution.py:228
  18.8 5.5 %collective-permute-start.4 = (f16[128,256]{1,0:T(8,128)(2,1)S(1)}, f16[128,256]{1,0:T(8,128)(2,1)S(1)}, u32[]{:S(2)}, u32[]{:S(2)}) collective-permute-start(f16[128,256]{1,0:T(8,128)(2,1)S(1)} %get-tuple-element.14), channel_id=1, source_target_pairs={{0,2},{1,3},{2,0},{3,1},{4,6},{5,7},{6,4},{7,5},{8,10},{9,11},{10,... | collective-permute-start | bytes 196616 | tf_op jit(solution)/shard_map/ppermute | solution.py:228
  19.5 4.8 %collective-permute-start.1 = (f16[128,256]{1,0:T(8,128)(2,1)S(1)}, f16[128,256]{1,0:T(8,128)(2,1)S(1)}, u32[]{:S(2)}, u32[]{:S(2)}) collective-permute-start(f16[128,256]{1,0:T(8,128)(2,1)S(1)} %fusion.18), channel_id=1, source_target_pairs={{0,1},{1,0},{2,3},{3,2},{4,5},{5,4},{6,7},{7,6},{8,9},{9,8},{10,11... | collective-permute-start | bytes 196616 | tf_op jit(solution)/shard_map/ppermute | solution.py:225
  25.1 3.6 %collective-permute-start.5 = (bf16[4,4096]{1,0:T(4,128)(2,1)S(1)}, bf16[4,4096]{1,0:T(4,128)(2,1)S(1)}, u32[]{:S(2)}, u32[]{:S(2)}) collective-permute-start(bf16[4,4096]{1,0:T(4,128)(2,1)S(1)} %convert_element_type.53), channel_id=1, source_target_pairs={{0,24},{8,16},{16,8},{24,0},{1,25},{9,17},{17,9},{25,1},{2,26},{10... | collective-permute-start | bytes 98312 | tf_op jit(solution)/shard_map/ppermute | solution.py:248
  29.9 3.1 %collective-permute-start.7 = (f32[4,512]{1,0:T(4,128)S(1)}, f32[4,512]{1,0:T(4,128)S(1)}, u32[]{:S(2)}, u32[]{:S(2)}) collective-permute-start(f32[4,512]{1,0:T(4,128)S(1)} %slice.60), channel_id=1, source_target_pairs={{0,24},{8,16},{16,8},{24,0},{1,25},{9,17},{17,9},{25,1},{2,26},{10... | collective-permute-start | bytes 24584 | tf_op jit(solution)/shard_map/ppermute | solution.py:251

commit v2 on v1

--- a/solution.py
+++ b/solution.py
@@ -11,10 +11,11 @@
 DATA_BOUND = 6.0
 IN_BOUND = 0.0625
 OUT_BOUND = 0.03125
+SMALLEST = 1e-36
 CONTRACT_LAST = (((1,), (1,)), ((), ()))
 VMEM_LIMIT = 20 * 1024 * 1024
-BLOCK = 1024
-FLIGHT = 5
+BLOCK = 1280
+FLIGHT = 4
 
 
 def code_scale(largest):
@@ -22,14 +23,14 @@
 
 
 def encode(value, scale):
-    root = jnp.sqrt(jnp.sqrt(jnp.abs(value))) * scale
-    return jnp.where(value < 0, -root, root)
+    size = jnp.maximum(jnp.abs(value), SMALLEST)
+    inverse = lax.rsqrt(size)
+    return value * scale * inverse * lax.rsqrt(size * inverse)
 
 
 def decode(code, scale):
     code = code * (1.0 / scale)
-    square = code * code
-    return jnp.where(code < 0, -square * square, square * square)
+    return (code * jnp.abs(code)) * (code * code)
 
 
 def project_kernel(offsets, away, first, scale, grads_hbm, inputs_hbm, out_factor, in_factor, *refs):

time: 33.7 us -> 33.2 us (0.985)
  transfers between devices with their start and end apart: 8 -> 8, of which waited for: 5 -> 5; matrix products, arithmetic and copies ran while one was open for 4% -> 3% of each run, Pallas kernels for 20% -> 21%
where the time goes in v2:
time: 33.2 us; the launch traced here: 33.1 us
  Pallas kernels  12.3 us (37%)
  starting transfers between devices  11.2 us (34%)
  waiting for transfers between devices  6.62 us (20%)
  matrix products  1.57 us (5%)
  other arithmetic  1.08 us (3%)
    pallas_call x2, Pallas kernels, project(): pl.pallas_call(functools.partial(project_kernel, tuple(offsets), away, fi...  10.8 us
    ppermute x3, starting transfers between devices, body(): lax.ppermute(leaving[n], 'tensor', [(i, i ^ 2 * m) for i in range(tensor_...  4.53 us
    ppermute x3, waiting for transfers between devices, body(): lax.ppermute(leaving[n], 'tensor', [(i, i ^ 2 * m) for i in range(tensor_...  3.02 us
    ppermute x1, starting transfers between devices, body(): got_far = lax.ppermute(coded[:-1].astype(jnp.float16), 'tensor', partner)  2.6 us
    ppermute x1, waiting for transfers between devices, body(): lax.ppermute(scores[k], 'dp', across[k])  2.14 us
    ppermute x1, starting transfers between devices, body(): got_near = lax.ppermute(coded_near.astype(jnp.float16), 'tensor', partner)  1.72 us
    pallas_call x1, Pallas kernels, hold(): pl.pallas_call(hold_kernel, in_specs=[pl.BlockSpec(memory_space=pl.ANY)]...  1.59 us
    dot_general x1, matrix products, body(): lax.dot_general(rows, hold(queries, twin), CONTRACT_LAST, preferred_eleme...  1.18 us
  transfers between devices with their start and end apart: 8, of which 5 were waited for; matrix products, arithmetic and copies ran while one was open for 3% of the time, Pallas kernels for 21%

profile of v2, /device:TPU:0, one launch (start us, length us, event | category | flops | bytes accessed | tf_op | source)
XLA Modules:
  0.0 33.1 jit_solution(1065299217360023973)
XLA Ops:
  0.0 5.5 %project.2 = (f32[4,128,256]{2,1,0:T(8,128)S(1)}, bf16[64,3584]{1,0:T(8,128)(2,1)S(1)}, bf16[64,1024]{1,0:T(8,128)(2,1)S(1)}, bf16[256,4096]{1,0:T(8,128)(2,1)S(1)}) custom-call(bf16[2048,3584]{1,0:T(8,128)(2,1)} %bitcast.20, bf16[2048,1024]{1,0:T(8,128)(2,1)} %bitcast.22, bf16[64,3584]{1,0:T(8,128)(2,1)} %bitcast.25, bf16[64,1024]{1,0:T(8,128)(2,1)} %bitcast.26, ...), custom_call_target="tpu_custom_call" | custom-call | flops 1207959552 | bytes 9437184 | tf_op jit(solution)/shard_map/project/pallas_call | solution.py:144
  5.5 0.5 %collective-permute-start.6 = (bf16[256,4096]{1,0:T(8,128)(2,1)S(1)}, bf16[256,4096]{1,0:T(8,128)(2,1)}, u32[]{:S(2)}, u32[]{:S(2)}) collective-permute-start(bf16[256,4096]{1,0:T(8,128)(2,1)S(1)} %get-tuple-element.12.ours), channel_id=1, source_target_pairs={{0,8},{8,0},{16,24},{24,16},{1,9},{9,1},{17,25},{25,17},{2,10},{10... | collective-permute-start | bytes 6291464 | tf_op jit(solution)/shard_map/ppermute | solution.py:245
  6.0 2.6 %collective-permute-start = (f16[3,128,256]{2,1,0:T(8,128)(2,1)S(1)}, f16[3,128,256]{2,1,0:T(8,128)(2,1)S(1)}, u32[]{:S(2)}, u32[]{:S(2)}) collective-permute-start(f16[3,128,256]{2,1,0:T(8,128)(2,1)S(1)} %slice_convert_fusion), channel_id=1, source_target_pairs={{0,1},{1,0},{2,3},{3,2},{4,5},{5,4},{6,7},{7,6},{8,9},{9,8},{10,11... | collective-permute-start | bytes 589832 | tf_op jit(solution)/shard_map/ppermute | solution.py:221
  8.6 0.0 copy-start
  8.6 0.0 copy-start.1
  8.6 5.3 %project.3 = f32[4,128,256]{2,1,0:T(8,128)S(1)} custom-call(bf16[2048,3584]{1,0:T(8,128)(2,1)} %bitcast.21, bf16[2048,1024]{1,0:T(8,128)(2,1)} %bitcast.23, bf16[64,3584]{1,0:T(8,128)(2,1)S(1)} %get-tuple-element.9.out_factor, bf16[64,1024]{1,0:T(8,128)(2,1)S(1)} %get-tuple-element.10.in_factor), custom_call_target="tpu_custom_call" | custom-call | flops 1207959552 | bytes 9437184 | tf_op jit(solution)/shard_map/project/pallas_call | solution.py:144
  13.9 0.3 collective-permute-done
  14.2 0.2 fusion.1
  14.5 3.9 %collective-permute-start.2 = (f16[128,256]{1,0:T(8,128)(2,1)S(1)}, f16[128,256]{1,0:T(8,128)(2,1)S(1)}, u32[]{:S(2)}, u32[]{:S(2)}) collective-permute-start(f16[128,256]{1,0:T(8,128)(2,1)S(1)} %get-tuple-element.13), channel_id=1, source_target_pairs={{0,6},{1,7},{2,4},{3,5},{4,2},{5,3},{6,0},{7,1},{8,14},{9,15},{10,... | collective-permute-start | bytes 196616 | tf_op jit(solution)/shard_map/ppermute | solution.py:229
  18.4 0.0 collective-permute-start.3
  18.4 0.6 %collective-permute-start.4 = (f16[128,256]{1,0:T(8,128)(2,1)S(1)}, f16[128,256]{1,0:T(8,128)(2,1)S(1)}, u32[]{:S(2)}, u32[]{:S(2)}) collective-permute-start(f16[128,256]{1,0:T(8,128)(2,1)S(1)} %get-tuple-element.14), channel_id=1, source_target_pairs={{0,2},{1,3},{2,0},{3,1},{4,6},{5,7},{6,4},{7,5},{8,10},{9,11},{10,... | collective-permute-start | bytes 196616 | tf_op jit(solution)/shard_map/ppermute | solution.py:229
  19.0 1.7 %collective-permute-start.1 = (f16[128,256]{1,0:T(8,128)(2,1)S(1)}, f16[128,256]{1,0:T(8,128)(2,1)S(1)}, u32[]{:S(2)}, u32[]{:S(2)}) collective-permute-start(f16[128,256]{1,0:T(8,128)(2,1)S(1)} %fusion.15), channel_id=1, source_target_pairs={{0,1},{1,0},{2,3},{3,2},{4,5},{5,4},{6,7},{7,6},{8,9},{9,8},{10,11... | collective-permute-start | bytes 196616 | tf_op jit(solution)/shard_map/ppermute | solution.py:226
  20.8 0.0 copy-done
  20.8 0.0 copy-done.1
  20.8 0.1 fusion.22
  20.8 0.2 collective-permute-done.2
  21.1 2.8 %collective-permute-done.3 = f16[128,256]{1,0:T(8,128)(2,1)S(1)} collective-permute-done((f16[128,256]{1,0:T(8,128)(2,1)S(1)}, f16[128,256]{1,0:T(8,128)(2,1)S(1)}, u32[]{:S(2)}, u32[]{:S(2)}) %collective-permute-start.3) | collective-permute-done | bytes 65568 | tf_op jit(solution)/shard_map/ppermute | solution.py:229
  23.8 0.0 collective-permute-done.4
  23.9 0.0 collective-permute-done.1
  23.9 0.1 fusion.10
  24.0 0.1 copy.10
  24.1 0.4 %convolution_convert_fusion = bf16[4,64,64]{2,1,0:T(8,128)(2,1)S(1)} fusion(f32[4,64,128]{2,1,0:T(8,128)S(1)} %bitcast.24, f32[4,64]{1,0:T(4,128)S(1)} %fusion.22), kind=kOutput, calls=%fused_computation | convolution fusion | flops 6324224 | bytes 296960 | tf_op jit(solution)/shard_map/esi,esj->eij/dot_general | solution.py:242
  24.5 0.1 convert_element_type.53
  24.6 0.8 %collective-permute-start.5 = (bf16[4,4096]{1,0:T(4,128)(2,1)S(1)}, bf16[4,4096]{1,0:T(4,128)(2,1)S(1)}, u32[]{:S(2)}, u32[]{:S(2)}) collective-permute-start(bf16[4,4096]{1,0:T(4,128)(2,1)S(1)} %convert_element_type.53), channel_id=1, source_target_pairs={{0,24},{8,16},{16,8},{24,0},{1,25},{9,17},{17,9},{25,1},{2,26},{10... | collective-permute-start | bytes 98312 | tf_op jit(solution)/shard_map/ppermute | solution.py:249
  25.4 0.0 collective-permute-done.6.theirs
  25.4 1.6 %hold.1 = bf16[512,4096]{1,0:T(8,128)(2,1)S(1)} custom-call(bf16[256,4096]{1,0:T(8,128)(2,1)S(1)} %get-tuple-element.12.ours, bf16[256,4096]{1,0:T(8,128)(2,1)} %collective-permute-done.6.theirs), custom_call_target="tpu_custom_call" | custom-call | bytes 4194304 | tf_op jit(solution)/shard_map/hold/pallas_call | solution.py:186
  27.0 1.2 %collective-permute-done.5 = bf16[4,4096]{1,0:T(4,128)(2,1)S(1)} collective-permute-done((bf16[4,4096]{1,0:T(4,128)(2,1)S(1)}, bf16[4,4096]{1,0:T(4,128)(2,1)S(1)}, u32[]{:S(2)}, u32[]{:S(2)}) %collective-permute-start.5) | collective-permute-done | bytes 32800 | tf_op jit(solution)/shard_map/ppermute | solution.py:249
  28.2 1.2 %fusion.16 = f32[8,512]{1,0:T(8,128)S(1)} fusion(bf16[512,4096]{1,0:T(8,128)(2,1)S(1)} %hold.1, bf16[4,4096]{1,0:T(4,128)(2,1)S(1)} %collective-permute-done.5, bf16[4,4096]{1,0:T(4,128)(2,1)S(1)} %convert_element_type.53), kind=kOutput, calls=%fused_computation.31 | convolution fusion | flops 33685504 | bytes 4276224 | tf_op jit(solution)/shard_map/dot_general | solution.py:250
  29.4 1.0 %collective-permute-start.7 = (f32[4,512]{1,0:T(4,128)S(1)}, f32[4,512]{1,0:T(4,128)S(1)}, u32[]{:S(2)}, u32[]{:S(2)}) collective-permute-start(f32[4,512]{1,0:T(4,128)S(1)} %slice.60), channel_id=1, source_target_pairs={{0,24},{8,16},{16,8},{24,0},{1,25},{9,17},{17,9},{25,1},{2,26},{10... | collective-permute-start | bytes 24584 | tf_op jit(solution)/shard_map/ppermute | solution.py:252
  30.3 2.1 %collective-permute-done.7 = f32[4,512]{1,0:T(4,128)S(1)} collective-permute-done((f32[4,512]{1,0:T(4,128)S(1)}, f32[4,512]{1,0:T(4,128)S(1)}, u32[]{:S(2)}, u32[]{:S(2)}) %collective-permute-start.7) | collective-permute-done | bytes 8224 | tf_op jit(solution)/shard_map/ppermute | solution.py:252
  32.5 0.6 %pad_maximum_fusion = f32[4,1024]{1,0:T(4,128)} fusion(f32[4,512]{1,0:T(4,128)S(1)} %get-tuple-element.17, f32[4,512]{1,0:T(4,128)S(1)} %get-tuple-element.16), kind=kLoop, calls=%fused_computation.36 | loop fusion | flops 4096 | bytes 32768 | tf_op jit(solution)/shard_map/concatenate | solution.py:260
  (5 shorter events, 0.1 us)
Async XLA Ops:
  5.5 19.9 %collective-permute-start.6 = (bf16[256,4096]{1,0:T(8,128)(2,1)S(1)}, bf16[256,4096]{1,0:T(8,128)(2,1)}, u32[]{:S(2)}, u32[]{:S(2)}) collective-permute-start(bf16[256,4096]{1,0:T(8,128)(2,1)S(1)} %get-tuple-element.12.ours), channel_id=1, source_target_pairs={{0,8},{8,0},{16,24},{24,16},{1,9},{9,1},{17,25},{25,17},{2,10},{10... | collective-permute-start | bytes 6291464 | tf_op jit(solution)/shard_map/ppermute | solution.py:245
  6.0 8.2 %collective-permute-start = (f16[3,128,256]{2,1,0:T(8,128)(2,1)S(1)}, f16[3,128,256]{2,1,0:T(8,128)(2,1)S(1)}, u32[]{:S(2)}, u32[]{:S(2)}) collective-permute-start(f16[3,128,256]{2,1,0:T(8,128)(2,1)S(1)} %slice_convert_fusion), channel_id=1, source_target_pairs={{0,1},{1,0},{2,3},{3,2},{4,5},{5,4},{6,7},{7,6},{8,9},{9,8},{10,11... | collective-permute-start | bytes 589832 | tf_op jit(solution)/shard_map/ppermute | solution.py:221
  8.6 12.1 %copy-start = (s32[4]{0:T(128)S(1)}, s32[4]{0:T(128)}, u32[]{:S(2)}) copy-start(s32[4]{0:T(128)} %param.11) | copy-start | bytes 52
  8.6 12.1 %copy-start.1 = (s32[4]{0:T(128)S(1)}, s32[4]{0:T(128)}, u32[]{:S(2)}) copy-start(s32[4]{0:T(128)} %param.12) | copy-start | bytes 52
  14.5 6.6 %collective-permute-start.2 = (f16[128,256]{1,0:T(8,128)(2,1)S(1)}, f16[128,256]{1,0:T(8,128)(2,1)S(1)}, u32[]{:S(2)}, u32[]{:S(2)}) collective-permute-start(f16[128,256]{1,0:T(8,128)(2,1)S(1)} %get-tuple-element.13), channel_id=1, source_target_pairs={{0,6},{1,7},{2,4},{3,5},{4,2},{5,3},{6,0},{7,1},{8,14},{9,15},{10,... | collective-permute-start | bytes 196616 | tf_op jit(solution)/shard_map/ppermute | solution.py:229
  18.4 5.5 %collective-permute-start.3 = (f16[128,256]{1,0:T(8,128)(2,1)S(1)}, f16[128,256]{1,0:T(8,128)(2,1)S(1)}, u32[]{:S(2)}, u32[]{:S(2)}) collective-permute-start(f16[128,256]{1,0:T(8,128)(2,1)S(1)} %get-tuple-element.15), channel_id=1, source_target_pairs={{0,4},{1,5},{2,6},{3,7},{4,0},{5,1},{6,2},{7,3},{8,12},{9,13},{10,... | collective-permute-start | bytes 196616 | tf_op jit(solution)/shard_map/ppermute | solution.py:229
  18.4 5.5 %collective-permute-start.4 = (f16[128,256]{1,0:T(8,128)(2,1)S(1)}, f16[128,256]{1,0:T(8,128)(2,1)S(1)}, u32[]{:S(2)}, u32[]{:S(2)}) collective-permute-start(f16[128,256]{1,0:T(8,128)(2,1)S(1)} %get-tuple-element.14), channel_id=1, source_target_pairs={{0,2},{1,3},{2,0},{3,1},{4,6},{5,7},{6,4},{7,5},{8,10},{9,11},{10,... | collective-permute-start | bytes 196616 | tf_op jit(solution)/shard_map/ppermute | solution.py:229
  19.0 4.8 %collective-permute-start.1 = (f16[128,256]{1,0:T(8,128)(2,1)S(1)}, f16[128,256]{1,0:T(8,128)(2,1)S(1)}, u32[]{:S(2)}, u32[]{:S(2)}) collective-permute-start(f16[128,256]{1,0:T(8,128)(2,1)S(1)} %fusion.15), channel_id=1, source_target_pairs={{0,1},{1,0},{2,3},{3,2},{4,5},{5,4},{6,7},{7,6},{8,9},{9,8},{10,11... | collective-permute-start | bytes 196616 | tf_op jit(solution)/shard_map/ppermute | solution.py:226
  24.6 3.6 %collective-permute-start.5 = (bf16[4,4096]{1,0:T(4,128)(2,1)S(1)}, bf16[4,4096]{1,0:T(4,128)(2,1)S(1)}, u32[]{:S(2)}, u32[]{:S(2)}) collective-permute-start(bf16[4,4096]{1,0:T(4,128)(2,1)S(1)} %convert_element_type.53), channel_id=1, source_target_pairs={{0,24},{8,16},{16,8},{24,0},{1,25},{9,17},{17,9},{25,1},{2,26},{10... | collective-permute-start | bytes 98312 | tf_op jit(solution)/shard_map/ppermute | solution.py:249
  29.4 3.1 %collective-permute-start.7 = (f32[4,512]{1,0:T(4,128)S(1)}, f32[4,512]{1,0:T(4,128)S(1)}, u32[]{:S(2)}, u32[]{:S(2)}) collective-permute-start(f32[4,512]{1,0:T(4,128)S(1)} %slice.60), channel_id=1, source_target_pairs={{0,24},{8,16},{16,8},{24,0},{1,25},{9,17},{17,9},{25,1},{2,26},{10... | collective-permute-start | bytes 24584 | tf_op jit(solution)/shard_map/ppermute | solution.py:252
